TPU v7x, 32 devices: a whole 2x2x4 slice. The times are simulated.
32 devices in a mesh: strings: 2 (over y), ka: 4 (over x, core), coef: 4 (over z).
Axes of the slice: x: 2, y: 2, z: 4, core: 2. Of those that a mesh axis runs over, the one named last changes fastest.
Arguments:
- wavefunctions: float32 [8, 49152, 384], P(('strings', 'ka'), 'coef'), parts along dimension 0, may hold values from -8 to 8
Outputs:
- transported: float32 [8, 49152, 384], P(('strings', 'ka'), 'coef'), parts along dimension 0
There are 2 independent parts, one for each index of `strings`. A program takes and returns all parts, laid end to end along the dimension named above; each array names one. Nothing has to cross between parts.
All inputs are finite; a program needn't handle non-finite values.
Results may differ from a plain program's by a relative error of at most 0.0003.
Values sent between devices are 32-bit elements; how exact they have to be, the bound alone decides.
A program may use at most 128 MiB of HBM per device.

v0:
```python
import jax
import jax.numpy as jnp
from jax import lax
from jax.sharding import PartitionSpec as P

G = 49152
NB = 384
NS_ITERS = 3


def shifted(block, axis, distance):
    devices = range(lax.axis_size(axis))
    route = [((i - distance) % len(devices), i) for i in devices]
    return lax.ppermute(block, axis, route)


def newton_step(iterate, gram_matrix):
    return 1.5 * iterate - 0.5 * jnp.einsum(
        "kia,kaj->kij", iterate, gram_matrix, precision=lax.Precision.HIGHEST
    )


def polar_full(margins):
    norm_scale = jnp.sqrt(NB * jnp.mean(margins * margins, axis=(1, 2)) + 1e-06)
    iterate = margins / norm_scale[:, None, None]
    for iteration in range(NS_ITERS):
        gram_matrix = jnp.einsum("kai,kaj->kij", iterate, iterate, precision=lax.Precision.HIGHEST)
        iterate = newton_step(iterate, gram_matrix)
    return iterate


def combine(earlier, later):
    return jnp.dot(earlier, later, precision=lax.Precision.HIGHEST)


def on_device(wavefunctions):
    local_points = wavefunctions.shape[0]
    carried = shifted(wavefunctions[local_points - 1], "ka", 1)
    first_pair = jnp.dot(carried.T, wavefunctions[0], precision=lax.Precision.HIGHEST)[None]
    partial_value = first_pair / G
    margins = lax.psum(partial_value, "coef")
    unitary = polar_full(margins)
    running = [unitary[0]]
    local_total = running[-1]
    identity = jnp.eye(NB, dtype=jnp.float32)
    gathered_products = lax.all_gather(local_total[None], "ka", axis=0, tiled=True)
    position = lax.axis_index("ka")

    def multiply_next(index_k, product):
        return combine(product, gathered_products[index_k])

    before = lax.fori_loop(0, position, multiply_next, identity)
    transports = jnp.stack(
        [combine(before, partial_product) for partial_product in running], axis=0
    )
    return jnp.einsum("kgj,kij->kgi", wavefunctions, transports, precision=lax.Precision.HIGHEST)


def solution(mesh):
    placed = (P(("strings", "ka"), "coef", None),)
    return jax.shard_map(
        on_device,
        mesh=mesh,
        in_specs=placed,
        out_specs=P(("strings", "ka"), "coef", None),
        check_vma=False,
    )
```

profile of v0, /device:TPU:7, one launch (start us, length us, event | category | flops | bytes accessed | tf_op | source)
XLA Modules:
  0.0 393.9 jit_solution(6581767508643108041)
XLA Ops:
  6.5 0.0 all-reduce.2.cloned.1.call-start
  6.5 0.8 collective-permute-start
  7.4 203.1 %collective-permute-done = f32[12288,384]{1,0:T(8,128)S(1)} collective-permute-done((f32[12288,384]{1,0:T(8,128)}, f32[12288,384]{1,0:T(8,128)S(1)}, u32[]{:S(2)}, u32[]{:S(2)}) %collective-permute-start) | collective-permute-done | bytes 18874400 | tf_op jit(solution)/shard_map/ppermute | solution.py:14
  210.4 33.9 %fusion.6 = f32[1,384,384]{2,1,0:T(8,128)} fusion(f32[12288,384]{1,0:T(8,128)S(1)} %collective-permute-done, f32[1,12288,384]{2,1,0:T(8,128)} %param.3), kind=kOutput, calls=%fused_computation.12 | convolution fusion | flops 21743419392 | bytes 38338560 | tf_op jit(solution)/shard_map/dot_general | solution.py:39
  244.3 0.0 all-reduce.2.cloned.1.call-update
  244.3 0.2 all-gather.2.cloned.1.call-start
  244.6 41.5 %all-reduce.2.cloned.1.call-done = f32[1,384,384]{2,1,0:T(8,128)} async-done(((f32[1,384,384]{2,1,0:T(8,128)}), f32[1,384,384]{2,1,0:T(8,128)}) %all-reduce.2.cloned.1.call-update) | async-done | bytes 589840 | tf_op jit(solution)/shard_map/psum | solution.py:41
  286.0 1.8 multiply_reduce_fusion
  288.5 2.6 fusion.18
  291.1 2.5 multiply_subtract_fusion
  293.6 1.3 fusion.15
  294.9 1.3 fusion.8
  296.2 1.3 fusion.12
  297.5 2.1 fusion.7
  299.6 0.0 all-gather.2.cloned.1.call-update
  299.7 23.8 %all-gather.2.cloned.1.call-done = f32[4,384,384]{2,1,0:T(8,128)} async-done(((f32[1,384,384]{2,1,0:T(8,128)}), f32[4,384,384]{2,1,0:T(8,128)}) %all-gather.2.cloned.1.call-update) | async-done | bytes 2359312 | tf_op jit(solution)/shard_map/all_gather | solution.py:46
  323.5 7.6 %while.10 = (s32[]{:T(128)}, f32[384,384]{0,1:T(8,128)S(1)}, s32[]{:T(128)}, f32[4,384,384]{2,1,0:T(8,128)}, s32[]{:T(128)}, /*index=5*/s32[]{:T(128)}, s32[]{:T(128)}) while((s32[]{:T(128)}, f32[384,384]{0,1:T(8,128)S(1)}, s32[]{:T(128)}, f32[4,384,384]{2,1,0:T(8,128)}, s32[]{:T(128)}, /*index=5*/s32[]{:T(128)}, s32[]{:T(128)}) %tuple.18), condition=%wide.region_3.0_spmd, body=%wide.region_2.0_spmd.sunk | while | flops 679477248 | bytes 2949243 | solution.py:52
  323.5 2.4 convolution_bitcast_fusion.3
  326.0 2.4 convolution_bitcast_fusion.3
  328.5 2.4 convolution_bitcast_fusion.3
  331.1 2.4 fusion.9
  333.5 34.9 %convolution_bitcast_fusion.1 = f32[1,12288,384]{1,2,0:T(8,128)} fusion(f32[384,384]{1,0:T(8,128)S(1)} %fusion.9, f32[1,12288,384]{2,1,0:T(8,128)} %param.3), kind=kOutput, calls=%fused_computation.4 | convolution fusion | flops 21743271936 | bytes 38338560 | tf_op jit(solution)/shard_map/kgj,kij->kgi/dot_general | solution.py:56
  368.4 18.6 %copy.3 = f32[1,12288,384]{2,1,0:T(8,128)} copy(f32[1,12288,384]{1,2,0:T(8,128)} %convolution_bitcast_fusion.1) | data formatting | bytes 37748736 | tf_op jit(solution)/shard_map/kgj,kij->kgi/dot_general | solution.py:56
  (4 shorter events, 0.2 us)
Async XLA Ops:
  6.5 279.5 %all-reduce.2.cloned.1.call-start = ((), (), s32[]{:S(2)}) async-start(), calls=%async_computation | async-start | bytes 1179648 | tf_op jit(solution)/shard_map/psum | solution.py:41
  6.5 203.9 %collective-permute-start = (f32[12288,384]{1,0:T(8,128)}, f32[12288,384]{1,0:T(8,128)S(1)}, u32[]{:S(2)}, u32[]{:S(2)}) collective-permute-start(f32[12288,384]{1,0:T(8,128)} %bitcast.61), channel_id=1, source_target_pairs={{12,0},{0,4},{4,8},{8,12},{13,1},{1,5},{5,9},{9,13},{14,2},{2,6},{... | collective-permute-start | bytes 56623112 | tf_op jit(solution)/shard_map/ppermute | solution.py:14
  244.3 79.2 %all-gather.2.cloned.1.call-start = ((), (), s32[]{:S(2)}) async-start(), calls=%async_computation.1 | async-start | bytes 2949120 | tf_op jit(solution)/shard_map/all_gather | solution.py:46
Sparse Core Ops, SparseCore 0:
  244.4 41.5 all-reduce.1
  299.8 23.6 all-gather.1
where the time goes:
time: 394 us
  waiting for transfers between devices  268 us (68%)
  matrix products  89.4 us (23%)
  local copies, waits for them, and re-layouts  18.7 us (5%)
  between operations  14.2 us (4%)
    ppermute x1, waiting for transfers between devices, shifted(): return lax.ppermute(block, axis, route)  203 us
    psum x1, waiting for transfers between devices, on_device(): margins = lax.psum(partial_value, 'coef')  41.5 us
    dot_general x1, matrix products, on_device(): jnp.einsum('kgj,kij->kgi', wavefunctions, transports, precision=lax.Preci...  34.9 us
    dot_general x1, matrix products, on_device(): jnp.dot(carried.T, wavefunctions[0], precision=lax.Precision.HIGHEST)[None]  33.9 us
    all_gather x1, waiting for transfers between devices, on_device(): lax.all_gather(local_total[None], 'ka', axis=0, tiled=True)  23.8 us
    dot_general x1, local copies, waits for them, and re-layouts, on_device(): jnp.einsum('kgj,kij->kgi', wavefunctions, transports, precision=lax.Preci...  18.6 us
    dot_general x4, matrix products, combine(): return jnp.dot(earlier, later, precision=lax.Precision.HIGHEST)  9.58 us
  transfers between devices with their start and end apart: 3, of which 3 were waited for; matrix products, arithmetic and copies ran while one was open for 0% of the time, Pallas kernels for 0%

commit v1 on v0

v1 whole, which is shorter than its diff:
```python
import functools

import jax
import jax.numpy as jnp
from jax import lax
from jax.experimental import pallas as pl
from jax.experimental.pallas import tpu as pltpu
from jax.sharding import PartitionSpec as P

G = 49152
NB = 384
NS_ITERS = 3
MESH = pl.DeviceIdType.MESH
MIB = 1024 * 1024


def split(x):
    high = x.astype(jnp.bfloat16)
    low = (x - high.astype(jnp.float32)).astype(jnp.bfloat16)
    return high, low


def dot3(a, b, dims):
    a_high, a_low = split(a)
    b_high, b_low = split(b)
    dot = functools.partial(
        lax.dot_general, dimension_numbers=(dims, ((), ())), preferred_element_type=jnp.float32
    )
    return dot(a_high, b_high) + (dot(a_low, b_high) + dot(a_high, b_low))


def matmul(a, b):
    return dot3(a, b, ((1,), (0,)))


def polar(margin):
    scale = jnp.sqrt(NB * jnp.mean(margin * margin, keepdims=True) + 1e-06)
    iterate = margin / scale
    for _ in range(NS_ITERS):
        gram = dot3(iterate, iterate, ((0,), (0,)))
        iterate = 1.5 * iterate - 0.5 * matmul(iterate, gram)
    return iterate


def unitary_kernel(n, part_ref, unitary_ref, arrived, full, send1, recv1, send2, recv2):
    me = lax.axis_index("coef")
    rows = part_ref.shape[0] // n
    peers = [lax.rem(me + d, n) for d in range(n)]

    def own(device):
        return pl.ds(pl.multiple_of(device * rows, 8), rows)

    barrier = pltpu.get_barrier_semaphore()
    for d in range(1, n):
        pl.semaphore_signal(barrier, inc=1, device_id={"coef": peers[d]}, device_id_type=MESH)
    pl.semaphore_wait(barrier, n - 1)

    scatter, gather = [], []
    for d in range(1, n):
        copy = pltpu.make_async_remote_copy(
            src_ref=part_ref.at[own(peers[d])], dst_ref=arrived.at[d],
            send_sem=send1.at[d], recv_sem=recv1.at[d],
            device_id={"coef": peers[d]}, device_id_type=MESH,
        )
        copy.start()
        scatter.append(copy)
    total = part_ref[own(me), :]
    for d in range(1, n):
        scatter[d - 1].wait_recv()
        total += arrived[d]
    full[own(me), :] = total
    for d in range(1, n):
        copy = pltpu.make_async_remote_copy(
            src_ref=full.at[own(me)], dst_ref=full.at[own(me)],
            send_sem=send2.at[d], recv_sem=recv2.at[d],
            device_id={"coef": peers[d]}, device_id_type=MESH,
        )
        copy.start()
        gather.append(copy)
    for d in range(1, n):
        gather[d - 1].wait_recv()
    for copy in scatter + gather:
        copy.wait_send()
    unitary_ref[...] = polar(full[...] / G)


def unitary_of(part, n):
    rows, columns = part.shape
    return pl.pallas_call(
        functools.partial(unitary_kernel, n),
        out_shape=jax.ShapeDtypeStruct(part.shape, jnp.float32),
        in_specs=[pl.BlockSpec(memory_space=pltpu.VMEM)],
        out_specs=pl.BlockSpec(memory_space=pltpu.VMEM),
        scratch_shapes=[
            pltpu.VMEM((n, rows // n, columns), jnp.float32),
            pltpu.VMEM((rows, columns), jnp.float32),
        ] + [pltpu.SemaphoreType.DMA((n,))] * 4,
        compiler_params=pltpu.CompilerParams(
            collective_id=0, has_side_effects=True, vmem_limit_bytes=24 * MIB
        ),
    )(part)


def transport_kernel(psi_ref, product_ref, out_ref, weights):
    @pl.when(pl.program_id(0) == 0)
    def _():
        high, low = split(product_ref[...].T)
        weights[...] = jnp.concatenate([high, high, low], axis=0)

    high, low = split(psi_ref[...])
    out_ref[...] = jnp.dot(
        jnp.concatenate([high, low, high], axis=1), weights[...],
        preferred_element_type=jnp.float32,
    )


def transport(psi, product):
    rows, columns = psi.shape
    block = 1024 if rows % 1024 == 0 else rows
    return pl.pallas_call(
        transport_kernel,
        grid=(rows // block,),
        out_shape=jax.ShapeDtypeStruct(psi.shape, jnp.float32),
        in_specs=[
            pl.BlockSpec((block, columns), lambda i: (i, 0)),
            pl.BlockSpec((columns, columns), lambda i: (0, 0)),
        ],
        out_specs=pl.BlockSpec((block, columns), lambda i: (i, 0)),
        scratch_shapes=[pltpu.VMEM((3 * columns, columns), jnp.bfloat16)],
        compiler_params=pltpu.CompilerParams(vmem_limit_bytes=32 * MIB),
    )(psi, product)


def on_device(wavefunctions):
    psi = wavefunctions[0]
    n_ka, n_coef = lax.axis_size("ka"), lax.axis_size("coef")
    rows = psi.shape[0]
    chunks = 8
    size = rows // chunks
    route = [((i - 1) % n_ka, i) for i in range(n_ka)]
    part = None
    blocks = [psi[c * size:(c + 1) * size] for c in range(chunks)]
    carried = [lax.ppermute(block, "ka", route) for block in blocks]
    for earlier, block in zip(carried, blocks):
        term = jnp.dot(earlier.T, block, precision=lax.Precision.HIGH)
        part = term if part is None else part + term
    if NB % (8 * n_coef) == 0:
        unitary = unitary_of(part, n_coef)
    else:
        unitary = polar(lax.psum(part, "coef") / G)
    unitaries = lax.all_gather(unitary, "ka", axis=0)
    position = lax.axis_index("ka")
    product = lax.fori_loop(
        1, position + 1,
        lambda k, total: jnp.dot(total, unitaries[k], precision=lax.Precision.HIGHEST),
        unitaries[0],
    )
    return transport(psi, product)[None]


def solution(mesh):
    placed = (P(("strings", "ka"), "coef", None),)
    return jax.shard_map(
        on_device,
        mesh=mesh,
        in_specs=placed,
        out_specs=P(("strings", "ka"), "coef", None),
        check_vma=False,
    )
```

time: 394 us -> 330 us (0.84)
  matrix products: 89.4 us -> 24.6 us
  waiting for transfers between devices: 268 us -> 206 us
  Pallas kernels: 0 us -> 53.3 us
  starting transfers between devices: 1.04 us -> 10.2 us
    dot_general x12 -> x11, matrix products: 89.4 us -> 24.6 us  [the longest x8 17.4 us: on_device(): term = jnp.dot(earlier.T, block, precision=lax.Precision.HIGH)]
    pallas_call x0 -> x2, Pallas kernels: none -> 53.3 us  [the longest x1 34.5 us: unitary_of(): pl.pallas_call(functools.partial(unitary_kernel, n), out_shape=jax.ShapeD...]
    psum x1 -> x0, waiting for transfers between devices: 41.5 us -> none  [on_device(): margins = lax.psum(partial_value, 'coef')]
    ppermute x1 -> x8, waiting for transfers between devices: 203 us -> 178 us  [on_device(): carried = [lax.ppermute(block, 'ka', route) for block in blocks]]
    dot_general x1 -> x0, local copies, waits for them, and re-layouts: 18.6 us -> none  [on_device(): jnp.einsum('kgj,kij->kgi', wavefunctions, transports, precision=lax.Preci...]
    slice x0 -> x2, local copies, waits for them, and re-layouts: none -> 15.6 us  [the longest x1 14.5 us: on_device(): blocks = [psi[c * size:(c + 1) * size] for c in range(chunks)]]
    ppermute x1 -> x8, starting transfers between devices: 0.82 us -> 10.2 us  [on_device(): carried = [lax.ppermute(block, 'ka', route) for block in blocks]]
    unnamed x0 -> x4, local copies, waits for them, and re-layouts: none -> 6.37 us
  transfers between devices with their start and end apart: 3 -> 9, of which waited for: 3 -> 9; matrix products, arithmetic and copies ran while one was open for 0% -> 5% of each run, Pallas kernels for 0% -> 0%
where the time goes in v1:
time: 330 us
  waiting for transfers between devices  206 us (62%)
  Pallas kernels  53.3 us (16%)
  matrix products  24.6 us (7%)
  local copies, waits for them, and re-layouts  22.6 us (7%)
  between operations  13.5 us (4%)
  starting transfers between devices  10.2 us (3%)
    ppermute x8, waiting for transfers between devices, on_device(): carried = [lax.ppermute(block, 'ka', route) for block in blocks]  178 us
    pallas_call x1, Pallas kernels, unitary_of(): pl.pallas_call(functools.partial(unitary_kernel, n), out_shape=jax.ShapeD...  34.5 us
    all_gather x1, waiting for transfers between devices, on_device(): unitaries = lax.all_gather(unitary, 'ka', axis=0)  27.4 us
    pallas_call x1, Pallas kernels, transport(): pl.pallas_call(transport_kernel, grid=(rows // block,), out_shape=jax.Sha...  18.8 us
    dot_general x8, matrix products, on_device(): term = jnp.dot(earlier.T, block, precision=lax.Precision.HIGH)  17.4 us
    slice x1, local copies, waits for them, and re-layouts, on_device(): blocks = [psi[c * size:(c + 1) * size] for c in range(chunks)]  14.5 us
    ppermute x8, starting transfers between devices, on_device(): carried = [lax.ppermute(block, 'ka', route) for block in blocks]  10.2 us
    dot_general x3, matrix products, on_device(): jnp.dot(total, unitaries[k], precision=lax.Precision.HIGHEST)  7.18 us
  transfers between devices with their start and end apart: 9, of which 9 were waited for; matrix products, arithmetic and copies ran while one was open for 5% of the time, Pallas kernels for 0%

profile of v1, /device:TPU:7, one launch (start us, length us, event | category | flops | bytes accessed | tf_op | source)
XLA Modules:
  0.0 330.2 jit_solution(6819598095327267608)
XLA Ops:
  6.5 14.5 %slice_bitcast_fusion.7 = (f32[1536,384]{1,0:T(8,128)}, f32[1536,384]{1,0:T(8,128)}, f32[1536,384]{1,0:T(8,128)}, f32[1536,384]{1,0:T(8,128)}, f32[1536,384]{1,0...) fusion(f32[1,12288,384]{2,1,0:T(8,128)} %param.3), kind=kLoop, calls=%fused_computation.11 | loop fusion | bytes 37748736 | tf_op jit(solution)/shard_map/slice | solution.py:142
  24.2 23.8 %collective-permute-done.2 = f32[1536,384]{1,0:T(8,128)S(1)} collective-permute-done((f32[1536,384]{1,0:T(8,128)}, f32[1536,384]{1,0:T(8,128)S(1)}, u32[]{:S(2)}, u32[]{:S(2)}) %collective-permute-start.2) | collective-permute-done | bytes 2359328 | tf_op jit(solution)/shard_map/ppermute | solution.py:143
  48.1 2.4 collective-permute-start.7
  50.4 22.9 %collective-permute-done.3 = f32[1536,384]{1,0:T(8,128)S(1)} collective-permute-done((f32[1536,384]{1,0:T(8,128)}, f32[1536,384]{1,0:T(8,128)S(1)}, u32[]{:S(2)}, u32[]{:S(2)}) %collective-permute-start.3) | collective-permute-done | bytes 2359328 | tf_op jit(solution)/shard_map/ppermute | solution.py:143
  73.3 2.4 collective-permute-start.1
  75.7 22.9 %collective-permute-done.4 = f32[1536,384]{1,0:T(8,128)S(1)} collective-permute-done((f32[1536,384]{1,0:T(8,128)}, f32[1536,384]{1,0:T(8,128)S(1)}, u32[]{:S(2)}, u32[]{:S(2)}) %collective-permute-start.4) | collective-permute-done | bytes 2359328 | tf_op jit(solution)/shard_map/ppermute | solution.py:143
  98.6 2.4 collective-permute-start
  101.0 2.1 fusion.10
  103.1 2.2 fusion.11
  107.4 16.5 %collective-permute-done.5 = f32[1536,384]{1,0:T(8,128)S(1)} collective-permute-done((f32[1536,384]{1,0:T(8,128)}, f32[1536,384]{1,0:T(8,128)S(1)}, u32[]{:S(2)}, u32[]{:S(2)}) %collective-permute-start.5) | collective-permute-done | bytes 2359328 | tf_op jit(solution)/shard_map/ppermute | solution.py:143
  126.0 23.1 %collective-permute-done.6 = f32[1536,384]{1,0:T(8,128)S(1)} collective-permute-done((f32[1536,384]{1,0:T(8,128)}, f32[1536,384]{1,0:T(8,128)S(1)}, u32[]{:S(2)}, u32[]{:S(2)}) %collective-permute-start.6) | collective-permute-done | bytes 2359328 | tf_op jit(solution)/shard_map/ppermute | solution.py:143
  151.3 23.1 %collective-permute-done.7 = f32[1536,384]{1,0:T(8,128)S(1)} collective-permute-done((f32[1536,384]{1,0:T(8,128)}, f32[1536,384]{1,0:T(8,128)S(1)}, u32[]{:S(2)}, u32[]{:S(2)}) %collective-permute-start.7) | collective-permute-done | bytes 2359328 | tf_op jit(solution)/shard_map/ppermute | solution.py:143
  174.5 2.3 fusion.15
  176.8 22.9 %collective-permute-done.1 = f32[1536,384]{1,0:T(8,128)S(1)} collective-permute-done((f32[1536,384]{1,0:T(8,128)}, f32[1536,384]{1,0:T(8,128)S(1)}, u32[]{:S(2)}, u32[]{:S(2)}) %collective-permute-start.1) | collective-permute-done | bytes 2359328 | tf_op jit(solution)/shard_map/ppermute | solution.py:143
  201.9 23.1 %collective-permute-done = f32[1536,384]{1,0:T(8,128)S(1)} collective-permute-done((f32[1536,384]{1,0:T(8,128)}, f32[1536,384]{1,0:T(8,128)S(1)}, u32[]{:S(2)}, u32[]{:S(2)}) %collective-permute-start) | collective-permute-done | bytes 2359328 | tf_op jit(solution)/shard_map/ppermute | solution.py:143
  225.0 2.3 fusion.8.part_ref
  227.3 34.5 %shard_map.17 = f32[384,384]{1,0:T(8,128)} custom-call(f32[384,384]{1,0:T(8,128)S(1)} %fusion.8.part_ref), custom_call_target="tpu_custom_call" | custom-call | tf_op jit(solution)/shard_map/pallas_call | solution.py:89
  261.8 27.4 %all-gather.3.cloned.1.call-done = f32[1536,384]{1,0:T(8,128)} async-done(((f32[384,384]{1,0:T(8,128)}), f32[1536,384]{1,0:T(8,128)}) %all-gather.3.cloned.1.call-update) | async-done | bytes 2359312 | tf_op jit(solution)/shard_map/all_gather | solution.py:151
  290.5 7.4 %while.10 = (s32[]{:T(128)}, f32[384,384]{0,1:T(8,128)S(1)}, s32[]{:T(128)}, f32[4,384,384]{2,1,0:T(8,128)}, s32[]{:T(128)}, /*index=5*/s32[]{:T(128)}, s32[]{:T(128)}) while((s32[]{:T(128)}, f32[384,384]{0,1:T(8,128)S(1)}, s32[]{:T(128)}, f32[4,384,384]{2,1,0:T(8,128)}, s32[]{:T(128)}, /*index=5*/s32[]{:T(128)}, s32[]{:T(128)}) %tuple.31), condition=%wide.region_1.0_spmd, body=%wide.region_0.0_spmd.sunk | while | flops 679477248 | bytes 2949235 | solution.py:153
  290.6 2.4 convolution_bitcast_fusion.2
  293.1 2.4 convolution_bitcast_fusion.2
  295.6 2.4 convolution_bitcast_fusion.2
  298.2 6.4 %copy-done.1 = f32[1,12288,384]{2,1,0:T(8,128)S(1)} copy-done((f32[1,12288,384]{2,1,0:T(8,128)S(1)}, f32[1,12288,384]{2,1,0:T(8,128)}, u32[]{:S(2)}) %copy-start.1) | copy-done | bytes 18874392
  304.6 18.8 %shard_map.18 = f32[12288,384]{1,0:T(8,128)} custom-call(f32[12288,384]{1,0:T(8,128)S(1)} %bitcast.47, f32[384,384]{1,0:T(8,128)S(1)} %copy.3.product_ref), custom_call_target="tpu_custom_call" | custom-call | tf_op jit(solution)/shard_map/pallas_call | solution.py:120
  (20 shorter events, 13.3 us)
Async XLA Ops:
  6.5 282.7 %all-gather.3.cloned.1.call-start = ((), (), s32[]{:S(2)}) async-start(), calls=%async_computation | async-start | bytes 2949120 | tf_op jit(solution)/shard_map/all_gather | solution.py:151
  6.5 94.5 %copy-start = (f32[1,12288,384]{2,1,0:T(8,128)S(1)}, f32[1,12288,384]{2,1,0:T(8,128)}, u32[]{:S(2)}) copy-start(f32[1,12288,384]{2,1,0:T(8,128)} %param.3) | copy-start | bytes 56623108
  21.1 27.0 %collective-permute-start.2 = (f32[1536,384]{1,0:T(8,128)}, f32[1536,384]{1,0:T(8,128)S(1)}, u32[]{:S(2)}, u32[]{:S(2)}) collective-permute-start(f32[1536,384]{1,0:T(8,128)} %get-tuple-element.45), channel_id=1, source_target_pairs={{12,0},{0,4},{4,8},{8,12},{13,1},{1,5},{5,9},{9,13},{14,2},{2,6},{... | collective-permute-start | bytes 7077896 | tf_op jit(solution)/shard_map/ppermute | solution.py:143
  22.0 51.4 %collective-permute-start.3 = (f32[1536,384]{1,0:T(8,128)}, f32[1536,384]{1,0:T(8,128)S(1)}, u32[]{:S(2)}, u32[]{:S(2)}) collective-permute-start(f32[1536,384]{1,0:T(8,128)} %get-tuple-element.44), channel_id=1, source_target_pairs={{12,0},{0,4},{4,8},{8,12},{13,1},{1,5},{5,9},{9,13},{14,2},{2,6},{... | collective-permute-start | bytes 7077896 | tf_op jit(solution)/shard_map/ppermute | solution.py:143
  22.0 76.6 %collective-permute-start.4 = (f32[1536,384]{1,0:T(8,128)}, f32[1536,384]{1,0:T(8,128)S(1)}, u32[]{:S(2)}, u32[]{:S(2)}) collective-permute-start(f32[1536,384]{1,0:T(8,128)} %get-tuple-element.43), channel_id=1, source_target_pairs={{12,0},{0,4},{4,8},{8,12},{13,1},{1,5},{5,9},{9,13},{14,2},{2,6},{... | collective-permute-start | bytes 7077896 | tf_op jit(solution)/shard_map/ppermute | solution.py:143
  23.6 100.3 %collective-permute-start.5 = (f32[1536,384]{1,0:T(8,128)}, f32[1536,384]{1,0:T(8,128)S(1)}, u32[]{:S(2)}, u32[]{:S(2)}) collective-permute-start(f32[1536,384]{1,0:T(8,128)} %get-tuple-element.42), channel_id=1, source_target_pairs={{12,0},{0,4},{4,8},{8,12},{13,1},{1,5},{5,9},{9,13},{14,2},{2,6},{... | collective-permute-start | bytes 7077896 | tf_op jit(solution)/shard_map/ppermute | solution.py:143
  23.6 125.6 %collective-permute-start.6 = (f32[1536,384]{1,0:T(8,128)}, f32[1536,384]{1,0:T(8,128)S(1)}, u32[]{:S(2)}, u32[]{:S(2)}) collective-permute-start(f32[1536,384]{1,0:T(8,128)} %get-tuple-element.48), channel_id=1, source_target_pairs={{12,0},{0,4},{4,8},{8,12},{13,1},{1,5},{5,9},{9,13},{14,2},{2,6},{... | collective-permute-start | bytes 7077896 | tf_op jit(solution)/shard_map/ppermute | solution.py:143
  48.1 126.4 %collective-permute-start.7 = (f32[1536,384]{1,0:T(8,128)}, f32[1536,384]{1,0:T(8,128)S(1)}, u32[]{:S(2)}, u32[]{:S(2)}) collective-permute-start(f32[1536,384]{1,0:T(8,128)} %get-tuple-element.47), channel_id=1, source_target_pairs={{12,0},{0,4},{4,8},{8,12},{13,1},{1,5},{5,9},{9,13},{14,2},{2,6},{... | collective-permute-start | bytes 7077896 | tf_op jit(solution)/shard_map/ppermute | solution.py:143
  73.3 126.4 %collective-permute-start.1 = (f32[1536,384]{1,0:T(8,128)}, f32[1536,384]{1,0:T(8,128)S(1)}, u32[]{:S(2)}, u32[]{:S(2)}) collective-permute-start(f32[1536,384]{1,0:T(8,128)} %get-tuple-element.46), channel_id=1, source_target_pairs={{12,0},{0,4},{4,8},{8,12},{13,1},{1,5},{5,9},{9,13},{14,2},{2,6},{... | collective-permute-start | bytes 7077896 | tf_op jit(solution)/shard_map/ppermute | solution.py:143
  98.6 126.4 %collective-permute-start = (f32[1536,384]{1,0:T(8,128)}, f32[1536,384]{1,0:T(8,128)S(1)}, u32[]{:S(2)}, u32[]{:S(2)}) collective-permute-start(f32[1536,384]{1,0:T(8,128)} %get-tuple-element.41), channel_id=1, source_target_pairs={{12,0},{0,4},{4,8},{8,12},{13,1},{1,5},{5,9},{9,13},{14,2},{2,6},{... | collective-permute-start | bytes 7077896 | tf_op jit(solution)/shard_map/ppermute | solution.py:143
  298.2 6.4 %copy-start.1 = (f32[1,12288,384]{2,1,0:T(8,128)S(1)}, f32[1,12288,384]{2,1,0:T(8,128)}, u32[]{:S(2)}) copy-start(f32[1,12288,384]{2,1,0:T(8,128)} %param.3) | copy-start | bytes 56623108
Sparse Core Ops, SparseCore 0:
  261.9 27.2 all-gather.2

commit v2 on v1

v2 whole, which is shorter than its diff:
```python
import functools

import jax
import jax.numpy as jnp
from jax import lax
from jax.experimental import pallas as pl
from jax.experimental.pallas import tpu as pltpu
from jax.sharding import PartitionSpec as P

G = 49152
NB = 384
NS_ITERS = 3
MESH = pl.DeviceIdType.MESH
MIB = 1024 * 1024


def split(x):
    high = x.astype(jnp.bfloat16)
    low = (x - high.astype(jnp.float32)).astype(jnp.bfloat16)
    return high, low


def dot3(a, b, dims):
    a_high, a_low = split(a)
    b_high, b_low = split(b)
    dot = functools.partial(
        lax.dot_general, dimension_numbers=(dims, ((), ())), preferred_element_type=jnp.float32
    )
    return dot(a_high, b_high) + (dot(a_low, b_high) + dot(a_high, b_low))


def matmul(a, b):
    return dot3(a, b, ((1,), (0,)))


def polar(margin):
    scale = jnp.sqrt(NB * jnp.mean(margin * margin, keepdims=True) + 1e-06)
    iterate = margin / scale
    for _ in range(NS_ITERS):
        gram = dot3(iterate, iterate, ((0,), (0,)))
        iterate = 1.5 * iterate - 0.5 * matmul(iterate, gram)
    return iterate


def product_kernel(
    n, n_coef, chunks, psi_ref, product_ref,
    carried, own, part, arrived, full, unitary, theirs, pair, earlier,
    load_sem, ring_send, ring_recv, send1, recv1, send2, recv2,
    swap_send, swap_recv, hop_send, hop_recv, pass_send, pass_recv,
):
    me, my_coef = lax.axis_index("ka"), lax.axis_index("coef")
    core, chip = lax.rem(me, 2), me // 2
    pairs = n // 2
    partner = me + 1 - 2 * core
    right = lax.rem(me + 1, n)
    size = psi_ref.shape[0] // chunks
    rows = NB // n_coef
    half = NB // 2
    peers = [lax.rem(my_coef + d, n_coef) for d in range(n_coef)]

    barrier = pltpu.get_barrier_semaphore()
    for d in range(1, n):
        pl.semaphore_signal(
            barrier, inc=1, device_id={"ka": lax.rem(me + d, n)}, device_id_type=MESH
        )
    for d in range(1, n_coef):
        pl.semaphore_signal(barrier, inc=1, device_id={"coef": peers[d]}, device_id_type=MESH)
    pl.semaphore_wait(barrier, n - 1 + n_coef - 1)

    def chunk(c):
        return pl.ds(pl.multiple_of(c * size, 8), size)

    def ring(c):
        return pltpu.make_async_remote_copy(
            src_ref=psi_ref.at[chunk(c)], dst_ref=carried.at[chunk(c)],
            send_sem=ring_send.at[c], recv_sem=ring_recv.at[c],
            device_id={"ka": right}, device_id_type=MESH,
        )

    def load(c):
        return pltpu.make_async_copy(psi_ref.at[chunk(c)], own.at[chunk(c)], load_sem.at[c])

    @pl.loop(0, chunks)
    def _(c):
        ring(c).start()
        load(c).start()

    part[...] = jnp.zeros_like(part)

    @pl.loop(0, chunks)
    def _(c):
        load(c).wait()
        ring(c).wait_recv()
        part[...] += dot3(carried[chunk(c), :], own[chunk(c), :], ((0,), (0,)))

    def own_rows(device):
        return pl.ds(pl.multiple_of(device * rows, 8), rows)

    def send(src, dst, send_sem, recv_sem, device):
        copy = pltpu.make_async_remote_copy(
            src_ref=src, dst_ref=dst, send_sem=send_sem, recv_sem=recv_sem,
            device_id=device, device_id_type=MESH,
        )
        copy.start()
        return copy

    scatter = [
        send(part.at[own_rows(peers[d])], arrived.at[d], send1.at[d], recv1.at[d],
             {"coef": peers[d]})
        for d in range(1, n_coef)
    ]
    total = part[own_rows(my_coef), :]
    for d in range(1, n_coef):
        scatter[d - 1].wait_recv()
        total += arrived[d]
    full[own_rows(my_coef), :] = total
    gather = [
        send(full.at[own_rows(my_coef)], full.at[own_rows(my_coef)], send2.at[d], recv2.at[d],
             {"coef": peers[d]})
        for d in range(1, n_coef)
    ]
    for copy in gather:
        copy.wait_recv()
    unitary[...] = polar(full[...] / G)

    swap = send(unitary, theirs, swap_send, swap_recv, {"ka": partner})
    swap.wait_recv()

    @pl.when(core == 0)
    def _():
        pair[...] = matmul(unitary[...], theirs[...])
        product_ref[...] = unitary[...]

    @pl.when(core == 1)
    def _():
        pair[...] = matmul(theirs[...], unitary[...])
        product_ref[...] = pair[...]

    mine = pl.ds(pl.multiple_of(core * half, 8), half)
    hops = [
        send(pair.at[mine], earlier.at[d, mine], hop_send.at[d], hop_recv.at[d],
             {"ka": 2 * lax.rem(chip + d, pairs) + core})
        for d in range(1, pairs)
    ]
    passes = []
    for d in range(1, pairs):
        hops[d - 1].wait_recv()
        passes.append(
            send(earlier.at[d, mine], earlier.at[d, mine], pass_send.at[d], pass_recv.at[d],
                 {"ka": partner})
        )
    for d in range(1, pairs):
        passes[d - 1].wait_recv()

        @pl.when(chip >= d)
        def _():
            product_ref[...] = matmul(earlier[d], product_ref[...])

    for copy in scatter + gather + [swap] + hops + passes:
        copy.wait_send()

    @pl.loop(0, chunks)
    def _(c):
        ring(c).wait_send()


def ordered_product(psi, n, n_coef, chunks):
    square = pltpu.VMEM((NB, NB), jnp.float32)
    dma = pltpu.SemaphoreType.DMA
    return pl.pallas_call(
        functools.partial(product_kernel, n, n_coef, chunks),
        out_shape=jax.ShapeDtypeStruct((NB, NB), jnp.float32),
        in_specs=[pl.BlockSpec(memory_space=pl.ANY)],
        out_specs=pl.BlockSpec(memory_space=pltpu.VMEM),
        scratch_shapes=[
            pltpu.VMEM(psi.shape, jnp.float32),
            pltpu.VMEM(psi.shape, jnp.float32),
            square,
            pltpu.VMEM((n_coef, NB // n_coef, NB), jnp.float32),
            square, square, square, square,
            pltpu.VMEM((n // 2, NB, NB), jnp.float32),
        ]
        + [dma((chunks,))] * 3
        + [dma((n_coef,))] * 4
        + [dma] * 2
        + [dma((n // 2,))] * 4,
        compiler_params=pltpu.CompilerParams(
            collective_id=0, has_side_effects=True, vmem_limit_bytes=58 * MIB
        ),
    )(psi)


def transport_kernel(psi_ref, product_ref, out_ref, weights):
    @pl.when(pl.program_id(0) == 0)
    def _():
        high, low = split(product_ref[...].T)
        weights[...] = jnp.concatenate([high, high, low], axis=0)

    high, low = split(psi_ref[...])
    out_ref[...] = jnp.dot(
        jnp.concatenate([high, low, high], axis=1), weights[...],
        preferred_element_type=jnp.float32,
    )


def transport(psi, product):
    rows, columns = psi.shape
    block = 1024 if rows % 1024 == 0 else rows
    return pl.pallas_call(
        transport_kernel,
        grid=(rows // block,),
        out_shape=jax.ShapeDtypeStruct(psi.shape, jnp.float32),
        in_specs=[
            pl.BlockSpec((block, columns), lambda i: (i, 0)),
            pl.BlockSpec((columns, columns), lambda i: (0, 0)),
        ],
        out_specs=pl.BlockSpec((block, columns), lambda i: (i, 0)),
        scratch_shapes=[pltpu.VMEM((3 * columns, columns), jnp.bfloat16)],
        compiler_params=pltpu.CompilerParams(vmem_limit_bytes=56 * MIB),
    )(psi, product)


def on_device(wavefunctions):
    psi = wavefunctions[0]
    n_ka, n_coef = lax.axis_size("ka"), lax.axis_size("coef")
    chunks = 16
    if n_ka % 2 == 0 and NB % (8 * n_coef) == 0 and psi.shape[0] % (8 * chunks) == 0:
        return transport(psi, ordered_product(psi, n_ka, n_coef, chunks))[None]
    route = [((i - 1) % n_ka, i) for i in range(n_ka)]
    carried = lax.ppermute(psi, "ka", route)
    part = jnp.dot(carried.T, psi, precision=lax.Precision.HIGH)
    unitary = polar(lax.psum(part, "coef") / G)
    unitaries = lax.all_gather(unitary, "ka", axis=0)
    product = lax.fori_loop(
        1, lax.axis_index("ka") + 1,
        lambda k, total: jnp.dot(total, unitaries[k], precision=lax.Precision.HIGHEST),
        unitaries[0],
    )
    return transport(psi, product)[None]


def solution(mesh):
    placed = (P(("strings", "ka"), "coef", None),)
    return jax.shard_map(
        on_device,
        mesh=mesh,
        in_specs=placed,
        out_specs=P(("strings", "ka"), "coef", None),
        check_vma=False,
    )
```

time: 330 us -> 266 us (0.81)
  Pallas kernels: 53.3 us -> 264 us
  waiting for transfers between devices: 206 us -> 0 us
  matrix products: 24.6 us -> 0 us
  local copies, waits for them, and re-layouts: 22.6 us -> 0 us
  between operations: 13.5 us -> 0.01 us
  starting transfers between devices: 10.2 us -> 0 us
    pallas_call x1, Pallas kernels: 34.5 us -> 240 us  [ordered_product(): pl.pallas_call(functools.partial(product_kernel, n, n_coef, chunks), out_...]
    ppermute x8 -> x0, waiting for transfers between devices: 178 us -> none  [on_device(): carried = [lax.ppermute(block, 'ka', route) for block in blocks]]
    all_gather x1 -> x0, waiting for transfers between devices: 27.4 us -> none  [on_device(): unitaries = lax.all_gather(unitary, 'ka', axis=0)]
    dot_general x11 -> x0, matrix products: 24.6 us -> none  [the longest x8 17.4 us: on_device(): term = jnp.dot(earlier.T, block, precision=lax.Precision.HIGH)]
    slice x2 -> x0, local copies, waits for them, and re-layouts: 15.6 us -> none  [the longest x1 14.5 us: on_device(): blocks = [psi[c * size:(c + 1) * size] for c in range(chunks)]]
    ppermute x8 -> x0, starting transfers between devices: 10.2 us -> none  [on_device(): carried = [lax.ppermute(block, 'ka', route) for block in blocks]]
    unnamed x4 -> x0, local copies, waits for them, and re-layouts: 6.37 us -> none
    pallas_call x1, Pallas kernels: 18.8 us -> 23.4 us  [transport(): pl.pallas_call(transport_kernel, grid=(rows // block,), out_shape=jax.Sha...]
  transfers between devices with their start and end apart: 9 -> 0, of which waited for: 9 -> 0; matrix products, arithmetic and copies ran while one was open for 5% -> 0% of each run, Pallas kernels for 0% -> 0%
where the time goes in v2:
time: 266 us; the launch traced here: 264 us
  Pallas kernels  264 us (99%)
    pallas_call x1, Pallas kernels, ordered_product(): pl.pallas_call(functools.partial(product_kernel, n, n_coef, chunks), out_...  240 us
    pallas_call x1, Pallas kernels, transport(): pl.pallas_call(transport_kernel, grid=(rows // block,), out_shape=jax.Sha...  23.4 us

profile of v2, /device:TPU:7, one launch (start us, length us, event | category | flops | bytes accessed | tf_op | source)
XLA Modules:
  0.0 263.7 jit_solution(4832325597285405520)
XLA Ops:
  0.0 240.3 %shard_map.17.product_ref = f32[384,384]{1,0:T(8,128)} custom-call(f32[12288,384]{1,0:T(8,128)} %bitcast.2), custom_call_target="tpu_custom_call" | custom-call | tf_op jit(solution)/shard_map/pallas_call | solution.py:170
  240.3 23.4 %shard_map.18 = f32[12288,384]{1,0:T(8,128)} custom-call(f32[12288,384]{1,0:T(8,128)} %bitcast.3, f32[384,384]{1,0:T(8,128)} %shard_map.17.product_ref), custom_call_target="tpu_custom_call" | custom-call | tf_op jit(solution)/shard_map/pallas_call | solution.py:209

commit v3 on v2

--- a/solution.py
+++ b/solution.py
@@ -12,6 +12,7 @@
 NS_ITERS = 3
 MESH = pl.DeviceIdType.MESH
 MIB = 1024 * 1024
+SLOTS = 4
 
 
 def split(x):
@@ -37,7 +38,7 @@
     scale = jnp.sqrt(NB * jnp.mean(margin * margin, keepdims=True) + 1e-06)
     iterate = margin / scale
     for _ in range(NS_ITERS):
-        gram = dot3(iterate, iterate, ((0,), (0,)))
+        gram = matmul(iterate.T, iterate)
         iterate = 1.5 * iterate - 0.5 * matmul(iterate, gram)
     return iterate
 
@@ -78,20 +79,26 @@
         )
 
     def load(c):
-        return pltpu.make_async_copy(psi_ref.at[chunk(c)], own.at[chunk(c)], load_sem.at[c])
+        slot = lax.rem(c, SLOTS)
+        return pltpu.make_async_copy(psi_ref.at[chunk(c)], own.at[slot], load_sem.at[slot])
 
     @pl.loop(0, chunks)
     def _(c):
         ring(c).start()
+
+    for c in range(SLOTS):
         load(c).start()
-
     part[...] = jnp.zeros_like(part)
 
     @pl.loop(0, chunks)
     def _(c):
         load(c).wait()
         ring(c).wait_recv()
-        part[...] += dot3(carried[chunk(c), :], own[chunk(c), :], ((0,), (0,)))
+        part[...] += dot3(carried[chunk(c), :], own[lax.rem(c, SLOTS)], ((0,), (0,)))
+
+        @pl.when(c + SLOTS < chunks)
+        def _():
+            load(c + SLOTS).start()
 
     def own_rows(device):
         return pl.ds(pl.multiple_of(device * rows, 8), rows)
@@ -170,22 +177,23 @@
     return pl.pallas_call(
         functools.partial(product_kernel, n, n_coef, chunks),
         out_shape=jax.ShapeDtypeStruct((NB, NB), jnp.float32),
-        in_specs=[pl.BlockSpec(memory_space=pl.ANY)],
+        in_specs=[pl.BlockSpec(memory_space=pltpu.HBM)],
         out_specs=pl.BlockSpec(memory_space=pltpu.VMEM),
         scratch_shapes=[
             pltpu.VMEM(psi.shape, jnp.float32),
-            pltpu.VMEM(psi.shape, jnp.float32),
+            pltpu.VMEM((SLOTS, psi.shape[0] // chunks, NB), jnp.float32),
             square,
             pltpu.VMEM((n_coef, NB // n_coef, NB), jnp.float32),
             square, square, square, square,
             pltpu.VMEM((n // 2, NB, NB), jnp.float32),
         ]
-        + [dma((chunks,))] * 3
+        + [dma((SLOTS,))]
+        + [dma((chunks,))] * 2
         + [dma((n_coef,))] * 4
         + [dma] * 2
         + [dma((n // 2,))] * 4,
         compiler_params=pltpu.CompilerParams(
-            collective_id=0, has_side_effects=True, vmem_limit_bytes=58 * MIB
+            collective_id=0, has_side_effects=True, vmem_limit_bytes=36 * MIB
         ),
     )(psi)
 
@@ -216,14 +224,14 @@
         ],
         out_specs=pl.BlockSpec((block, columns), lambda i: (i, 0)),
         scratch_shapes=[pltpu.VMEM((3 * columns, columns), jnp.bfloat16)],
-        compiler_params=pltpu.CompilerParams(vmem_limit_bytes=56 * MIB),
+        compiler_params=pltpu.CompilerParams(vmem_limit_bytes=24 * MIB),
     )(psi, product)
 
 
 def on_device(wavefunctions):
     psi = wavefunctions[0]
     n_ka, n_coef = lax.axis_size("ka"), lax.axis_size("coef")
-    chunks = 16
+    chunks = 32
     if n_ka % 2 == 0 and NB % (8 * n_coef) == 0 and psi.shape[0] % (8 * chunks) == 0:
         return transport(psi, ordered_product(psi, n_ka, n_coef, chunks))[None]
     route = [((i - 1) % n_ka, i) for i in range(n_ka)]

time: 266 us -> 260 us (0.977)
  Pallas kernels: 264 us -> 258 us
    pallas_call x1, Pallas kernels: 23.4 us -> 18.8 us  [transport(): pl.pallas_call(transport_kernel, grid=(rows // block,), out_shape=jax.Sha...]
where the time goes in v3:
time: 260 us; the launch traced here: 258 us
  Pallas kernels  258 us (99%)
    pallas_call x1, Pallas kernels, ordered_product(): pl.pallas_call(functools.partial(product_kernel, n, n_coef, chunks), out_...  239 us
    pallas_call x1, Pallas kernels, transport(): pl.pallas_call(transport_kernel, grid=(rows // block,), out_shape=jax.Sha...  18.8 us

profile of v3, /device:TPU:7, one launch (start us, length us, event | category | flops | bytes accessed | tf_op | source)
XLA Modules:
  0.0 258.2 jit_solution(8222788167408140749)
XLA Ops:
  0.0 0.0 copy-start
  0.0 239.4 %shard_map.17.product_ref = f32[384,384]{1,0:T(8,128)S(1)} custom-call(f32[12288,384]{1,0:T(8,128)} %bitcast.2), custom_call_target="tpu_custom_call" | custom-call | tf_op jit(solution)/shard_map/pallas_call | solution.py:177
  239.4 0.0 copy-done
  239.4 18.8 %shard_map.18 = f32[12288,384]{1,0:T(8,128)} custom-call(f32[12288,384]{1,0:T(8,128)S(1)} %bitcast.3, f32[384,384]{1,0:T(8,128)S(1)} %shard_map.17.product_ref), custom_call_target="tpu_custom_call" | custom-call | tf_op jit(solution)/shard_map/pallas_call | solution.py:217
Async XLA Ops:
  0.0 239.4 %copy-start = (f32[1,12288,384]{2,1,0:T(8,128)S(1)}, f32[1,12288,384]{2,1,0:T(8,128)}, u32[]{:S(2)}) copy-start(f32[1,12288,384]{2,1,0:T(8,128)} %param.1) | copy-start | bytes 56623108
